TPU v7x, 1024 devices: a whole 8x8x8 slice. The times are simulated.
1024 devices in a mesh: expert: 64 (over z, y), dp: 16 (over x, core).
Axes of the slice: x: 8, y: 8, z: 8, core: 2. Of those that a mesh axis runs over, the one named last changes fastest.
Arguments:
- grad_out: bfloat16 [16, 8192, 2048], P('dp', 'expert'), may hold values from -6 to 6
- router_logits: float32 [16, 8192, 64], P('dp', 'expert'), may hold values from -8 to 8
- choices: int32 [16, 64, 256], P('dp'), may hold values from 0 to 8191, as said below
- pre_act: bfloat16 [16, 64, 256, 1024], P('dp', 'expert'), may hold values from -6 to 6
- w_down: bfloat16 [64, 1024, 2048], P('expert'), may hold values from -0.125 to 0.125
- w_up: bfloat16 [64, 2048, 1024], P('expert'), may hold values from -0.1875 to 0.1875
Outputs:
- grad_tokens: bfloat16 [16, 8192, 2048], P('dp', 'expert')
- grad_logits: float32 [16, 8192, 64], P('dp', 'expert')
- down_grad: bfloat16 [64, 1024, 2048], P('expert', 'dp')
Inputs may be any that keep to these rules, and one draw needn't show every extreme that they name: Each block choices[g, e, :] lists 256 different tokens of group g. Of one block, at most 6 tokens lie in one device's tokens j * 128 to (j + 1) * 128 - 1, and in every block some device supplies exactly 6.
All inputs are finite; a program needn't handle non-finite values.
Results may differ from a plain program's by a relative error of at most 0.022.
Values may be sent and summed in bfloat16 or wider, within the bound.
A program may use at most 64 MiB of HBM per device.

v0:
```python
import jax
import jax.numpy as jnp
from jax import lax
from jax.experimental import pallas as pl
from jax.experimental.pallas import tpu as pltpu
from jax.sharding import PartitionSpec as P

ROOT_TWO_PI = 0.7978845608028654
CUBIC = 0.044715
MESH = pl.DeviceIdType.MESH

SIDE = 8
PEERS = 64
RING = 8
TOK = 128
WIDTH = 2048
FF = 1024
CAP = 256
SLOTS = 6
FLAT = PEERS * SLOTS
SUB = 16
GROUP = 16
GROUPS = PEERS // GROUP
ROWS = GROUP * SLOTS
BLOCK = FF // (2 * RING)
HALF = BLOCK // 2

F32 = jnp.float32
BF16 = jnp.bfloat16
I32 = jnp.int32


def contract(left, right, left_dim, right_dim):
    return lax.dot_general(
        left, right, (((left_dim,), (right_dim,)), ((), ())), preferred_element_type=F32
    )


def gelu_pair(values):
    inner_arg = ROOT_TWO_PI * (values + CUBIC * values * values * values)
    tanh_part = jnp.tanh(inner_arg)
    hidden = 0.5 * values * (1.0 + tanh_part)
    slope_vals = 0.5 * (1.0 + tanh_part) + 0.5 * values * (
        1.0 - tanh_part * tanh_part
    ) * ROOT_TWO_PI * (1.0 + 3.0 * CUBIC * values * values)
    return hidden, slope_vals


def iota(shape, dim):
    return lax.broadcasted_iota(I32, shape, dim)


def kernel(
    choices_ref, logits_ref, rows_ref, act_ref, down_hbm, up_hbm,
    tok_out, logit_out, down_out,
    w_down, w_up, stage, send_buf, recv_buf, back_buf, ret_buf,
    gate_send, gate_recv, grad_send, grad_recv,
    landing, tok_of_row, rows2d, scaled, hidden, slope, hidden_t, pre_grad,
    partial, pair_recv, pair_sum, ring_send, ring_recv,
    weight_sem,
    send_sem, recv_sem, gate_send_sem, gate_recv_sem,
    back_send_sem, back_recv_sem, grad_send_sem, grad_recv_sem,
    pair_send_sem, pair_recv_sem, ring_send_sem, ring_recv_sem,
):
    me = lax.axis_index("expert")
    data = lax.axis_index("dp")
    my_z, my_y = lax.div(me, SIDE), lax.rem(me, SIDE)
    my_x, core = lax.div(data, 2), lax.rem(data, 2)
    sign = 1 - 2 * core

    def partner(step, way):
        dz = lax.rem(3 * step, SIDE)
        dy = lax.rem(2 * step + lax.div(step, SIDE), SIDE)
        z = lax.rem(my_z + way * dz + SIDE, SIDE)
        y = lax.rem(my_y + way * dy + SIDE, SIDE)
        return z * SIDE + y

    def step_between(origin, target):
        dz = jnp.bitwise_and(sign * ((target >> 3) - (origin >> 3)), SIDE - 1)
        dy = jnp.bitwise_and(sign * ((target & 7) - (origin & 7)), SIDE - 1)
        low = jnp.bitwise_and(3 * dz, SIDE - 1)
        return jnp.bitwise_and(dy - 2 * low, SIDE - 1) * SIDE + low

    right = lax.rem(my_x + 1, RING) * 2 + core
    left = lax.rem(my_x + RING - 1, RING) * 2 + core
    sibling = my_x * 2 + 1 - core

    copy_down = pltpu.make_async_copy(down_hbm, w_down, weight_sem.at[0])
    copy_up = pltpu.make_async_copy(up_hbm, w_up, weight_sem.at[1])
    copy_down.start()
    copy_up.start()

    barrier = pltpu.get_barrier_semaphore()

    def greet(step, carry):
        pl.semaphore_signal(
            barrier, inc=1, device_id={"expert": lax.rem(me + step, PEERS)}, device_id_type=MESH
        )
        return carry

    lax.fori_loop(1, PEERS, greet, 0)
    for other in (left, right, sibling):
        pl.semaphore_signal(barrier, inc=1, device_id={"dp": other}, device_id_type=MESH)

    chosen = choices_ref[...]
    mine = (chosen >> 7) == me
    token = jnp.where(mine, (chosen & (TOK - 1)) + 1, 0)
    lane = iota((PEERS, CAP), 1)
    before = jnp.where(mine, 1, 0)
    shift = 1
    while shift < CAP:
        before = before + jnp.where(lane >= shift, pltpu.roll(before, shift, 1), 0)
        shift *= 2
    column = iota((PEERS, GROUPS * 128), 1)
    within = column & 127
    step_in = (within * 43) >> 8
    slot_in = within - SLOTS * step_in
    at_step = step_between(me, iota((PEERS, GROUPS * 128), 0)) == (column >> 7) * GROUP + step_in
    at_step = at_step & (within < ROWS)
    spread = jnp.zeros((PEERS, GROUPS * 128), I32)
    for k in range(SLOTS):
        token_k = jnp.sum(jnp.where(before == k + 1, token, 0), axis=1, keepdims=True)
        spread = spread + jnp.where(at_step & (slot_in == k), token_k, 0)
    token_row = jnp.sum(spread, axis=0, keepdims=True) - 1
    landing_f = jnp.where(token_row == iota((TOK, GROUPS * 128), 0), 1.0, 0.0)
    landing[...] = landing_f.astype(BF16)

    expert_step = step_between(me, iota((PEERS, PEERS), 0)) == iota((PEERS, PEERS), 1)
    expert_to_step = jnp.where(expert_step, 1.0, 0.0).astype(BF16)
    eye = jnp.where(iota((TOK, TOK), 0) == iota((TOK, TOK), 1), 1.0, 0.0).astype(BF16)
    gates = 1.0 / (1.0 + jnp.exp(-logits_ref[...]))
    by_step = jnp.dot(gates.astype(BF16), expert_to_step, preferred_element_type=F32)
    gate_send[:, 0, :] = contract(by_step.astype(BF16), eye, 0, 0)

    def tiles(row, count):
        return pl.ds(pl.multiple_of(row * SUB, SUB), count * SUB)

    def gather(g):
        pick = jnp.transpose(landing_f[:, g * 128:(g + 1) * 128]).astype(BF16)[0:ROWS]
        for n in range(WIDTH // 256):
            rows_n = jnp.dot(
                pick, rows_ref[:, n * 256:(n + 1) * 256], preferred_element_type=F32
            )
            for h in range(2):
                stage[pl.ds(g * ROWS * SUB + 2 * n + h, ROWS, stride=SUB), :] = rows_n[
                    :, h * 128:(h + 1) * 128
                ]

    def pack(row):
        return stage[tiles(row, SLOTS), :].astype(BF16).reshape(SLOTS, SUB, 128)

    def push(step, carry):
        block = pl.ds(step * SLOTS, SLOTS)
        send_buf[block] = pack(step * SLOTS)
        p = partner(step, sign)
        g = lax.div(step, GROUP)
        pltpu.make_async_remote_copy(
            src_ref=gate_send.at[pl.ds(step, 1)], dst_ref=gate_recv.at[pl.ds(step, 1)],
            send_sem=gate_send_sem, recv_sem=gate_recv_sem.at[g],
            device_id={"expert": p}, device_id_type=MESH,
        ).start()
        pltpu.make_async_remote_copy(
            src_ref=send_buf.at[block], dst_ref=recv_buf.at[block],
            send_sem=send_sem, recv_sem=recv_sem.at[g],
            device_id={"expert": p}, device_id_type=MESH,
        ).start()
        return carry

    gather(0)
    pl.semaphore_wait(barrier, PEERS + 2)
    lax.fori_loop(1, GROUP, push, 0)
    for g in range(1, GROUPS):
        gather(g)
        lax.fori_loop(g * GROUP, (g + 1) * GROUP, push, 0)
    recv_buf[0:SLOTS] = pack(0)
    gate_recv[0:1] = gate_send[0:1]

    own = iota((PEERS, CAP), 0) == me
    own_row = jnp.sum(jnp.where(own, chosen, 0), axis=0, keepdims=True)
    here, there = iota((CAP, CAP), 0), iota((CAP, CAP), 1)
    own_col = jnp.sum(jnp.where(here == there, own_row, 0), axis=1, keepdims=True)
    src_row, src_col = own_row >> 7, own_col >> 7
    loc_col = own_col & (TOK - 1)
    rank_col = jnp.sum(
        jnp.where((src_col == src_row) & (there < here), 1, 0), axis=1, keepdims=True
    )
    step_col = step_between(src_col, me)
    column_col = (step_col >> 4) * 128 + (step_col & (GROUP - 1)) * SLOTS + rank_col
    arrival = jnp.where(
        column_col == iota((CAP, GROUPS * 128), 1), 1.0, 0.0
    )
    onehot_loc = jnp.where(loc_col == iota((CAP, TOK), 1), 1.0, 0.0).astype(BF16)
    for g in range(GROUPS):
        block = slice(g * ROWS, (g + 1) * ROWS)
        place = jnp.transpose(arrival[:, g * 128:(g + 1) * 128]).astype(BF16)[0:ROWS]
        tok_of_row[block, :] = jnp.dot(place, onehot_loc, preferred_element_type=F32)
        for n in range(FF // 256):
            columns = slice(n * 256, (n + 1) * 256)
            act = jnp.dot(place, act_ref[:, columns], preferred_element_type=F32)
            hidden_n, slope_n = gelu_pair(act)
            hidden[block, columns] = hidden_n
            slope[block, columns] = slope_n
    for n in range(FF // 128):
        columns = slice(n * 128, (n + 1) * 128)
        hidden_t[columns, :] = jnp.transpose(hidden[:, columns]).astype(BF16)
    row_step = lax.div(iota((ROWS, GROUP), 0), SLOTS) == iota((ROWS, GROUP), 1)
    row_to_step = jnp.where(row_step, 1.0, 0.0).astype(BF16)

    def wait_bytes(source, target, sem, count):
        pltpu.make_async_copy(
            source.at[pl.ds(0, count)], target.at[pl.ds(0, count)], sem
        ).wait()

    def await_rows(g):
        steps = GROUP - 1 if g == 0 else GROUP
        wait_bytes(gate_send, gate_recv, gate_recv_sem.at[g], steps)
        wait_bytes(send_buf, recv_buf, recv_sem.at[g], steps * SLOTS)

    def unpack(source, g):
        for j in range(8):
            count = ROWS // 8
            stage[j * count * SUB:(j + 1) * count * SUB, :] = (
                source[g * ROWS + j * count:g * ROWS + (j + 1) * count]
                .astype(F32)
                .reshape(count * SUB, 128)
            )

    def arrive(g):
        block = slice(g * ROWS, (g + 1) * ROWS)
        unpack(recv_buf, g)
        gate_rows = jnp.dot(
            row_to_step,
            gate_recv[g * GROUP:(g + 1) * GROUP, 0, :].astype(BF16),
            preferred_element_type=F32,
        )
        gate_col = jnp.sum(gate_rows * tok_of_row[block, :], axis=1, keepdims=True)
        for c in range(SUB):
            columns = slice(c * 128, (c + 1) * 128)
            chunk = stage[pl.ds(c, ROWS, stride=SUB), :]
            rows2d[block, columns] = chunk.astype(BF16)
            scaled[block, columns] = (gate_col * chunk).astype(BF16)
        return gate_col

    def work(g, gate_col):
        block = slice(g * ROWS, (g + 1) * ROWS)
        gate_grad = jnp.zeros((ROWS, 1), F32)
        for n in range(FF // 256):
            columns = slice(n * 256, (n + 1) * 256)
            back = contract(rows2d[block, :], w_down[columns, :], 1, 1)
            gate_grad = gate_grad + jnp.sum(back * hidden[block, columns], axis=1, keepdims=True)
            pre_grad[:, columns] = (gate_col * back * slope[block, columns]).astype(BF16)
        marked = (gate_grad.astype(BF16).astype(F32) * tok_of_row[block, :]).astype(BF16)
        grad_send[g * GROUP:(g + 1) * GROUP, 0, :] = contract(row_to_step, marked, 0, 0)
        for n in range(WIDTH // 256):
            rows_n = contract(pre_grad[...], w_up[n * 256:(n + 1) * 256, :], 1, 1)
            for h in range(2):
                stage[pl.ds(2 * n + h, ROWS, stride=SUB), :] = rows_n[:, h * 128:(h + 1) * 128]
        for j in range(8):
            count = ROWS // 8
            back_buf[g * ROWS + j * count:g * ROWS + (j + 1) * count] = (
                stage[j * count * SUB:(j + 1) * count * SUB, :]
                .astype(BF16)
                .reshape(count, SUB, 128)
            )

    def push_back(step, carry):
        block = pl.ds(step * SLOTS, SLOTS)
        p = partner(step, -sign)
        g = lax.div(step, GROUP)
        pltpu.make_async_remote_copy(
            src_ref=grad_send.at[pl.ds(step, 1)], dst_ref=grad_recv.at[pl.ds(step, 1)],
            send_sem=grad_send_sem, recv_sem=grad_recv_sem.at[g],
            device_id={"expert": p}, device_id_type=MESH,
        ).start()
        pltpu.make_async_remote_copy(
            src_ref=back_buf.at[block], dst_ref=ret_buf.at[block],
            send_sem=back_send_sem, recv_sem=back_recv_sem.at[g],
            device_id={"expert": p}, device_id_type=MESH,
        ).start()
        return carry

    for g in range(GROUPS - 1):
        await_rows(g)
        gate_col = arrive(g)
        if g == 0:
            copy_down.wait()
            copy_up.wait()
        work(g, gate_col)
    lax.fori_loop(1, GROUP, push_back, 0)
    await_rows(GROUPS - 1)
    lax.fori_loop(GROUP, (GROUPS - 1) * GROUP, push_back, 0)
    gate_col = arrive(GROUPS - 1)

    for n in range(WIDTH // 256):
        columns = slice(n * 256, (n + 1) * 256)
        partial[:, columns] = jnp.dot(
            hidden_t[...], scaled[:, columns], preferred_element_type=F32
        ).astype(BF16)

    def pair_copy(b):
        return pltpu.make_async_remote_copy(
            src_ref=partial.at[pl.ds((2 * b + 1 - core) * BLOCK, BLOCK)],
            dst_ref=pair_recv.at[pl.ds(b * BLOCK, BLOCK)],
            send_sem=pair_send_sem, recv_sem=pair_recv_sem.at[b],
            device_id={"dp": sibling}, device_id_type=MESH,
        )

    for b in range(RING):
        pair_copy(b).start()
    work(GROUPS - 1, gate_col)
    lax.fori_loop((GROUPS - 1) * GROUP, PEERS, push_back, 0)
    ret_buf[0:SLOTS] = back_buf[0:SLOTS]
    grad_recv[0:1] = grad_send[0:1]

    for b in range(RING):
        pair_copy(b).wait_recv()
        both = pair_recv[b * BLOCK:(b + 1) * BLOCK, :].astype(F32) + partial[
            pl.ds((2 * b + core) * BLOCK, BLOCK), :
        ].astype(F32)
        pair_sum[b * BLOCK:(b + 1) * BLOCK, :] = both.astype(BF16)

    streams = ((0, 1, 4), (0, -1, 3), (1, 1, 3), (1, -1, 4))
    slot_of = {}
    for stream, (half, way, steps) in enumerate(streams):
        for s in range(1, steps + 1):
            slot_of[stream, s] = len(slot_of)

    def ring_copy(stream, s):
        half, way, steps = streams[stream]
        slot = slot_of[stream, s]
        block = lax.rem(my_x + way * (steps + 1 - s) + RING, RING)
        place = pl.ds(block * BLOCK + half * HALF, HALF)
        return place, slot, pltpu.make_async_remote_copy(
            src_ref=pair_sum.at[place] if s == 1 else ring_send.at[slot],
            dst_ref=ring_recv.at[slot],
            send_sem=ring_send_sem.at[slot], recv_sem=ring_recv_sem.at[slot],
            device_id={"dp": right if way == 1 else left}, device_id_type=MESH,
        )

    def ring_step(s):
        for stream, (half, way, steps) in enumerate(streams):
            if s > steps:
                continue
            place, slot, copy = ring_copy(stream, s)
            if s > 1:
                ring_copy(stream, s - 1)[2].wait_recv()
                total = ring_recv[slot_of[stream, s - 1]].astype(F32) + pair_sum[place, :].astype(F32)
                ring_send[slot] = total.astype(BF16)
            copy.start()

    def land(g):
        steps = GROUP - 1 if g == 0 else GROUP
        wait_bytes(grad_send, grad_recv, grad_recv_sem.at[g], steps)
        wait_bytes(back_buf, ret_buf, back_recv_sem.at[g], steps * SLOTS)
        unpack(ret_buf, g)
        for c in range(SUB):
            rows2d[g * ROWS:(g + 1) * ROWS, c * 128:(c + 1) * 128] = stage[
                pl.ds(c, ROWS, stride=SUB), :
            ].astype(BF16)

    ring_step(1)
    ring_step(2)
    land(0)
    ring_step(3)
    land(1)
    ring_step(4)
    for half in range(2):
        place = pl.ds(my_x * BLOCK + half * HALF, HALF)
        total = pair_sum[place, :].astype(F32)
        for stream, (of_half, way, steps) in enumerate(streams):
            if of_half == half:
                ring_copy(stream, steps)[2].wait_recv()
                total = total + ring_recv[slot_of[stream, steps]].astype(F32)
        down_out[half * HALF:(half + 1) * HALF, :] = total.astype(BF16)
    land(2)
    land(3)
    for n in range(WIDTH // 256):
        columns = slice(n * 256, (n + 1) * 256)
        total = jnp.zeros((TOK, 256), F32)
        for g in range(GROUPS):
            total = total + jnp.dot(
                landing[:, g * 128:g * 128 + ROWS],
                rows2d[g * ROWS:(g + 1) * ROWS, columns],
                preferred_element_type=F32,
            )
        tok_out[:, columns] = total.astype(BF16)
    gates = 1.0 / (1.0 + jnp.exp(-logits_ref[...]))
    step_to_expert = jnp.where(
        step_between(me, iota((PEERS, PEERS), 1)) == iota((PEERS, PEERS), 0), 1.0, 0.0
    ).astype(BF16)
    picked_grad = contract(grad_recv[:, 0, :].astype(BF16), step_to_expert, 0, 0)
    logit_out[...] = picked_grad * gates * (1.0 - gates)

    others = FLAT - SLOTS
    wait_bytes(send_buf, recv_buf, send_sem, others)
    wait_bytes(gate_send, gate_recv, gate_send_sem, PEERS - 1)
    wait_bytes(back_buf, ret_buf, back_send_sem, others)
    wait_bytes(grad_send, grad_recv, grad_send_sem, PEERS - 1)
    wait_bytes(pair_sum, pair_recv, pair_send_sem, RING * BLOCK)
    for stream, s in slot_of:
        ring_copy(stream, s)[2].wait_send()


def on_device(grad_out, router_logits, choices, pre_act, w_down, w_up):
    vmem = pl.BlockSpec(memory_space=pltpu.VMEM)
    anywhere = pl.BlockSpec(memory_space=pl.ANY)
    dma = pltpu.SemaphoreType.DMA
    tokens, logits, down = pl.pallas_call(
        kernel,
        out_shape=(
            jax.ShapeDtypeStruct((TOK, WIDTH), BF16),
            jax.ShapeDtypeStruct((TOK, PEERS), F32),
            jax.ShapeDtypeStruct((BLOCK, WIDTH), BF16),
        ),
        in_specs=[vmem, vmem, vmem, vmem, anywhere, anywhere],
        out_specs=(vmem, vmem, vmem),
        scratch_shapes=[
            pltpu.VMEM((FF, WIDTH), BF16),
            pltpu.VMEM((WIDTH, FF), BF16),
            pltpu.VMEM((FLAT * SUB, 128), F32),
            pltpu.VMEM((FLAT, SUB, 128), BF16),
            pltpu.VMEM((FLAT, SUB, 128), BF16),
            pltpu.VMEM((FLAT, SUB, 128), BF16),
            pltpu.VMEM((FLAT, SUB, 128), BF16),
            pltpu.VMEM((PEERS, 1, TOK), F32),
            pltpu.VMEM((PEERS, 1, TOK), F32),
            pltpu.VMEM((PEERS, 1, TOK), F32),
            pltpu.VMEM((PEERS, 1, TOK), F32),
            pltpu.VMEM((TOK, GROUPS * 128), BF16),
            pltpu.VMEM((FLAT, TOK), F32),
            pltpu.VMEM((FLAT, WIDTH), BF16),
            pltpu.VMEM((FLAT, WIDTH), BF16),
            pltpu.VMEM((FLAT, FF), F32),
            pltpu.VMEM((FLAT, FF), F32),
            pltpu.VMEM((FF, FLAT), BF16),
            pltpu.VMEM((ROWS, FF), BF16),
            pltpu.VMEM((FF, WIDTH), BF16),
            pltpu.VMEM((RING * BLOCK, WIDTH), BF16),
            pltpu.VMEM((RING * BLOCK, WIDTH), BF16),
            pltpu.VMEM((14, HALF, WIDTH), BF16),
            pltpu.VMEM((14, HALF, WIDTH), BF16),
            dma((2,)),
            dma, dma((GROUPS,)), dma, dma((GROUPS,)),
            dma, dma((GROUPS,)), dma, dma((GROUPS,)),
            dma, dma((RING,)), dma((14,)), dma((14,)),
        ],
        compiler_params=pltpu.CompilerParams(
            collective_id=0, has_side_effects=True, vmem_limit_bytes=56 << 20
        ),
        cost_estimate=pl.CostEstimate(
            flops=3 * 2 * CAP * FF * WIDTH, bytes_accessed=12 << 20, transcendentals=CAP * FF
        ),
        name="expert_backward",
    )(choices[0], router_logits[0], grad_out[0], pre_act[0, 0], w_down[0], w_up[0])
    return tokens[None], logits[None], down[None]


def solution(mesh):
    return jax.shard_map(
        on_device,
        mesh=mesh,
        in_specs=(
            P("dp", "expert", None),
            P("dp", "expert", None),
            P("dp", None, None),
            P("dp", "expert", None, None),
            P("expert", None, None),
            P("expert", None, None),
        ),
        out_specs=(P("dp", "expert", None), P("dp", "expert", None), P("expert", "dp", None)),
        check_vma=False,
    )
```

profile of v0, /device:TPU:1, one launch (start us, length us, event | category | flops | bytes accessed | tf_op | source)
XLA Modules:
  0.0 106.2 jit_solution(2935896195514725655)
XLA Ops:
  0.6 1.5 %copy.9 = f32[1,128,64]{2,1,0:T(8,128)} copy(f32[1,128,64]{1,2,0:T(8,128)} %param.7) | data formatting | bytes 65536 | tf_op args[1]
  2.1 99.0 %expert_backward.1 = (bf16[128,2048]{1,0:T(8,128)(2,1)}, f32[128,64]{1,0:T(8,128)}, bf16[64,2048]{1,0:T(8,128)(2,1)}) custom-call(s32[64,256]{1,0:T(8,128)} %bitcast.17, f32[128,64]{1,0:T(8,128)} %bitcast.12, bf16[128,2048]{1,0:T(8,128)(2,1)} %bitcast.15, bf16[256,1024]{1,0:T(8,128)(2,1)} %bitcast.16, bf16[1024,2048]{1,0:T(8,128)(2,1)} %bitcast.13, ...), custom_call_target="tpu_custom_call" | custom-call | flops 3221225472 | bytes 12582912 | tf_op jit(solution)/shard_map/expert_backward/pallas_call | solution.py:408
  101.1 1.5 %copy.10 = f32[1,128,64]{1,2,0:T(8,128)} copy(f32[1,128,64]{2,1,0:T(8,128)} %bitcast.11) | data formatting | bytes 65536
  102.7 1.9 %copy.13 = bf16[1,128,2048]{2,1,0:T(8,128)(2,1)} copy(bf16[1,128,2048]{2,1,0:T(8,128)(2,1)} %bitcast.9) | data formatting | bytes 1048576
  104.6 1.7 %copy.14 = bf16[1,64,2048]{2,1,0:T(8,128)(2,1)} copy(bf16[1,64,2048]{2,1,0:T(8,128)(2,1)} %bitcast.10) | data formatting | bytes 524288
where the time goes:
time: 107 us; the launch traced here: 106 us
  Pallas kernels  99 us (93%)
  local copies, waits for them, and re-layouts  6.57 us (6%)
    pallas_call x1, Pallas kernels, on_device(): pl.pallas_call(kernel, out_shape=(jax.ShapeDtypeStruct((TOK, WIDTH), BF16...  99 us
    unnamed x4, local copies, waits for them, and re-layouts  6.57 us

commit v1 on v0

--- a/solution.py
+++ b/solution.py
@@ -127,10 +127,8 @@
 
     expert_step = step_between(me, iota((PEERS, PEERS), 0)) == iota((PEERS, PEERS), 1)
     expert_to_step = jnp.where(expert_step, 1.0, 0.0).astype(BF16)
-    eye = jnp.where(iota((TOK, TOK), 0) == iota((TOK, TOK), 1), 1.0, 0.0).astype(BF16)
     gates = 1.0 / (1.0 + jnp.exp(-logits_ref[...]))
-    by_step = jnp.dot(gates.astype(BF16), expert_to_step, preferred_element_type=F32)
-    gate_send[:, 0, :] = contract(by_step.astype(BF16), eye, 0, 0)
+    gate_send[:, 0, :] = contract(expert_to_step, gates.astype(BF16), 0, 0)
 
     def tiles(row, count):
         return pl.ds(pl.multiple_of(row * SUB, SUB), count * SUB)
@@ -200,9 +198,10 @@
             hidden_n, slope_n = gelu_pair(act)
             hidden[block, columns] = hidden_n
             slope[block, columns] = slope_n
-    for n in range(FF // 128):
-        columns = slice(n * 128, (n + 1) * 128)
-        hidden_t[columns, :] = jnp.transpose(hidden[:, columns]).astype(BF16)
+    for n in range(RING):
+        turned = jnp.transpose(hidden[:, n * 128:(n + 1) * 128]).astype(BF16)
+        hidden_t[pl.ds((1 - core) * (RING * BLOCK) + n * BLOCK, BLOCK), :] = turned[0:BLOCK]
+        hidden_t[pl.ds(core * (RING * BLOCK) + n * BLOCK, BLOCK), :] = turned[BLOCK:]
     row_step = lax.div(iota((ROWS, GROUP), 0), SLOTS) == iota((ROWS, GROUP), 1)
     row_to_step = jnp.where(row_step, 1.0, 0.0).astype(BF16)
 
@@ -288,36 +287,40 @@
         work(g, gate_col)
     lax.fori_loop(1, GROUP, push_back, 0)
     await_rows(GROUPS - 1)
-    lax.fori_loop(GROUP, (GROUPS - 1) * GROUP, push_back, 0)
     gate_col = arrive(GROUPS - 1)
 
-    for n in range(WIDTH // 256):
-        columns = slice(n * 256, (n + 1) * 256)
-        partial[:, columns] = jnp.dot(
-            hidden_t[...], scaled[:, columns], preferred_element_type=F32
-        ).astype(BF16)
-
-    def pair_copy(b):
+    def multiply(half):
+        rows = slice(half * RING * BLOCK, (half + 1) * RING * BLOCK)
+        for n in range(WIDTH // 256):
+            columns = slice(n * 256, (n + 1) * 256)
+            partial[rows, columns] = jnp.dot(
+                hidden_t[rows, :], scaled[:, columns], preferred_element_type=F32
+            ).astype(BF16)
+
+    away = (4, 3, -3, 2, -2, 1, -1, 0)
+
+    def pair_copy(j):
+        block = lax.rem(my_x + away[j] + RING, RING)
         return pltpu.make_async_remote_copy(
-            src_ref=partial.at[pl.ds((2 * b + 1 - core) * BLOCK, BLOCK)],
-            dst_ref=pair_recv.at[pl.ds(b * BLOCK, BLOCK)],
-            send_sem=pair_send_sem, recv_sem=pair_recv_sem.at[b],
+            src_ref=partial.at[pl.ds(block * BLOCK, BLOCK)],
+            dst_ref=pair_recv.at[pl.ds(block * BLOCK, BLOCK)],
+            send_sem=pair_send_sem, recv_sem=pair_recv_sem.at[j],
             device_id={"dp": sibling}, device_id_type=MESH,
         )
 
-    for b in range(RING):
-        pair_copy(b).start()
-    work(GROUPS - 1, gate_col)
-    lax.fori_loop((GROUPS - 1) * GROUP, PEERS, push_back, 0)
-    ret_buf[0:SLOTS] = back_buf[0:SLOTS]
-    grad_recv[0:1] = grad_send[0:1]
-
-    for b in range(RING):
-        pair_copy(b).wait_recv()
-        both = pair_recv[b * BLOCK:(b + 1) * BLOCK, :].astype(F32) + partial[
-            pl.ds((2 * b + core) * BLOCK, BLOCK), :
+    def pair_add(j):
+        pair_copy(j).wait_recv()
+        block = lax.rem(my_x + away[j] + RING, RING)
+        both = pair_recv[pl.ds(block * BLOCK, BLOCK), :].astype(F32) + partial[
+            pl.ds((RING + block) * BLOCK, BLOCK), :
         ].astype(F32)
-        pair_sum[b * BLOCK:(b + 1) * BLOCK, :] = both.astype(BF16)
+        pair_sum[pl.ds(block * BLOCK, BLOCK), :] = both.astype(BF16)
+
+    multiply(0)
+    for j in range(RING):
+        pair_copy(j).start()
+    multiply(1)
+    lax.fori_loop(GROUP, (GROUPS - 1) * GROUP, push_back, 0)
 
     streams = ((0, 1, 4), (0, -1, 3), (1, 1, 3), (1, -1, 4))
     slot_of = {}
@@ -358,12 +361,21 @@
                 pl.ds(c, ROWS, stride=SUB), :
             ].astype(BF16)
 
+    for j in range(3):
+        pair_add(j)
     ring_step(1)
+    work(GROUPS - 1, gate_col)
+    lax.fori_loop((GROUPS - 1) * GROUP, PEERS, push_back, 0)
+    ret_buf[0:SLOTS] = back_buf[0:SLOTS]
+    grad_recv[0:1] = grad_send[0:1]
+    for j in range(3, RING):
+        pair_add(j)
     ring_step(2)
     land(0)
     ring_step(3)
     land(1)
     ring_step(4)
+    land(2)
     for half in range(2):
         place = pl.ds(my_x * BLOCK + half * HALF, HALF)
         total = pair_sum[place, :].astype(F32)
@@ -372,7 +384,6 @@
                 ring_copy(stream, steps)[2].wait_recv()
                 total = total + ring_recv[slot_of[stream, steps]].astype(F32)
         down_out[half * HALF:(half + 1) * HALF, :] = total.astype(BF16)
-    land(2)
     land(3)
     for n in range(WIDTH // 256):
         columns = slice(n * 256, (n + 1) * 256)
@@ -388,7 +399,7 @@
     step_to_expert = jnp.where(
         step_between(me, iota((PEERS, PEERS), 1)) == iota((PEERS, PEERS), 0), 1.0, 0.0
     ).astype(BF16)
-    picked_grad = contract(grad_recv[:, 0, :].astype(BF16), step_to_expert, 0, 0)
+    picked_grad = contract(step_to_expert, grad_recv[:, 0, :].astype(BF16), 0, 0)
     logit_out[...] = picked_grad * gates * (1.0 - gates)
 
     others = FLAT - SLOTS
@@ -401,6 +412,19 @@
         ring_copy(stream, s)[2].wait_send()
 
 
+def hand_over(tokens, logits, down, tok_out, logit_out, down_out, sems):
+    copies = [
+        pltpu.make_async_copy(source, target, sems.at[i])
+        for i, (source, target) in enumerate(
+            ((tokens, tok_out), (logits, logit_out), (down, down_out))
+        )
+    ]
+    for copy in copies:
+        copy.start()
+    for copy in copies:
+        copy.wait()
+
+
 def on_device(grad_out, router_logits, choices, pre_act, w_down, w_up):
     vmem = pl.BlockSpec(memory_space=pltpu.VMEM)
     anywhere = pl.BlockSpec(memory_space=pl.ANY)
@@ -409,7 +433,7 @@
         kernel,
         out_shape=(
             jax.ShapeDtypeStruct((TOK, WIDTH), BF16),
-            jax.ShapeDtypeStruct((TOK, PEERS), F32),
+            jax.ShapeDtypeStruct((PEERS, TOK), F32),
             jax.ShapeDtypeStruct((BLOCK, WIDTH), BF16),
         ),
         in_specs=[vmem, vmem, vmem, vmem, anywhere, anywhere],
@@ -451,8 +475,17 @@
             flops=3 * 2 * CAP * FF * WIDTH, bytes_accessed=12 << 20, transcendentals=CAP * FF
         ),
         name="expert_backward",
-    )(choices[0], router_logits[0], grad_out[0], pre_act[0, 0], w_down[0], w_up[0])
-    return tokens[None], logits[None], down[None]
+    )(choices[0], router_logits[0].T, grad_out[0], pre_act[0, 0], w_down[0], w_up[0])
+    tokens, logits, down = pl.pallas_call(
+        hand_over,
+        out_shape=[jax.ShapeDtypeStruct(x.shape, x.dtype) for x in (tokens, logits, down)],
+        in_specs=[anywhere] * 3,
+        out_specs=[anywhere] * 3,
+        scratch_shapes=[dma((3,))],
+        compiler_params=pltpu.CompilerParams(vmem_limit_bytes=60 << 20),
+        name="hand_over",
+    )(tokens, logits, down)
+    return tokens[None], logits.T[None], down[None]
 
 
 def solution(mesh):

time: 107 us -> 126 us (1.18)
  Pallas kernels: 99 us -> 125 us
  local copies, waits for them, and re-layouts: 6.57 us -> 0 us
    pallas_call x0 -> x1, Pallas kernels: none -> 25.9 us  [on_device(): pl.pallas_call(hand_over, out_shape=[jax.ShapeDtypeStruct(x.shape, x.dtyp...]
    unnamed x4 -> x0, local copies, waits for them, and re-layouts: 6.57 us -> none
where the time goes in v1:
time: 126 us; the launch traced here: 125 us
  Pallas kernels  125 us (99%)
    pallas_call x1, Pallas kernels, on_device(): pl.pallas_call(kernel, out_shape=(jax.ShapeDtypeStruct((TOK, WIDTH), BF16...  98.6 us
    pallas_call x1, Pallas kernels, on_device(): pl.pallas_call(hand_over, out_shape=[jax.ShapeDtypeStruct(x.shape, x.dtyp...  25.9 us

profile of v1, /device:TPU:1, one launch (start us, length us, event | category | flops | bytes accessed | tf_op | source)
XLA Modules:
  0.0 125.3 jit_solution(4825939112719851299)
XLA Ops:
  0.6 98.6 %expert_backward.1 = (bf16[128,2048]{1,0:T(8,128)(2,1)}, f32[64,128]{1,0:T(8,128)}, bf16[64,2048]{1,0:T(8,128)(2,1)}) custom-call(s32[64,256]{1,0:T(8,128)} %bitcast.19, f32[64,128]{1,0:T(8,128)} %bitcast.20, bf16[128,2048]{1,0:T(8,128)(2,1)} %bitcast.15, bf16[256,1024]{1,0:T(8,128)(2,1)} %bitcast.16, bf16[1024,2048]{1,0:T(8,128)(2,1)} %bitcast.13, ...), custom_call_target="tpu_custom_call" | custom-call | flops 3221225472 | bytes 12582912 | tf_op jit(solution)/shard_map/expert_backward/pallas_call | solution.py:432
  99.2 25.9 %hand_over.1 = (bf16[128,2048]{1,0:T(8,128)(2,1)}, f32[64,128]{1,0:T(8,128)}, bf16[64,2048]{1,0:T(8,128)(2,1)}) custom-call(bf16[128,2048]{1,0:T(8,128)(2,1)} %get-tuple-element.9.tokens, f32[64,128]{1,0:T(8,128)} %get-tuple-element.10.logits, bf16[64,2048]{1,0:T(8,128)(2,1)} %get-tuple-element.11.down), custom_call_target="tpu_custom_call" | custom-call | tf_op jit(solution)/shard_map/hand_over/pallas_call | solution.py:479

commit v2 on v1

--- a/solution.py
+++ b/solution.py
@@ -51,9 +51,9 @@
 
 
 def kernel(
-    choices_ref, logits_ref, rows_ref, act_ref, down_hbm, up_hbm,
+    choices_hbm, logits_hbm, rows_hbm, act_hbm, down_hbm, up_hbm,
     tok_out, logit_out, down_out,
-    w_down, w_up, stage, send_buf, recv_buf, back_buf, ret_buf,
+    choices_ref, logits_ref, rows_ref, act_ref, w_down, w_up, tok_sum, stage, send_buf, recv_buf, back_buf, ret_buf,
     gate_send, gate_recv, grad_send, grad_recv,
     landing, tok_of_row, rows2d, scaled, hidden, slope, hidden_t, pre_grad,
     partial, pair_recv, pair_sum, ring_send, ring_recv,
@@ -85,11 +85,6 @@
     left = lax.rem(my_x + RING - 1, RING) * 2 + core
     sibling = my_x * 2 + 1 - core
 
-    copy_down = pltpu.make_async_copy(down_hbm, w_down, weight_sem.at[0])
-    copy_up = pltpu.make_async_copy(up_hbm, w_up, weight_sem.at[1])
-    copy_down.start()
-    copy_up.start()
-
     barrier = pltpu.get_barrier_semaphore()
 
     def greet(step, carry):
@@ -101,6 +96,18 @@
     lax.fori_loop(1, PEERS, greet, 0)
     for other in (left, right, sibling):
         pl.semaphore_signal(barrier, inc=1, device_id={"dp": other}, device_id_type=MESH)
+    loads = [
+        pltpu.make_async_copy(source, target, weight_sem.at[i])
+        for i, (source, target) in enumerate(
+            (
+                (choices_hbm, choices_ref), (logits_hbm, logits_ref), (rows_hbm, rows_ref),
+                (act_hbm, act_ref), (down_hbm, w_down), (up_hbm, w_up),
+            )
+        )
+    ]
+    for load in loads:
+        load.start()
+    loads[0].wait()
 
     chosen = choices_ref[...]
     mine = (chosen >> 7) == me
@@ -127,6 +134,7 @@
 
     expert_step = step_between(me, iota((PEERS, PEERS), 0)) == iota((PEERS, PEERS), 1)
     expert_to_step = jnp.where(expert_step, 1.0, 0.0).astype(BF16)
+    loads[1].wait()
     gates = 1.0 / (1.0 + jnp.exp(-logits_ref[...]))
     gate_send[:, 0, :] = contract(expert_to_step, gates.astype(BF16), 0, 0)
 
@@ -164,6 +172,7 @@
         ).start()
         return carry
 
+    loads[2].wait()
     gather(0)
     pl.semaphore_wait(barrier, PEERS + 2)
     lax.fori_loop(1, GROUP, push, 0)
@@ -188,6 +197,7 @@
         column_col == iota((CAP, GROUPS * 128), 1), 1.0, 0.0
     )
     onehot_loc = jnp.where(loc_col == iota((CAP, TOK), 1), 1.0, 0.0).astype(BF16)
+    loads[3].wait()
     for g in range(GROUPS):
         block = slice(g * ROWS, (g + 1) * ROWS)
         place = jnp.transpose(arrival[:, g * 128:(g + 1) * 128]).astype(BF16)[0:ROWS]
@@ -282,8 +292,8 @@
         await_rows(g)
         gate_col = arrive(g)
         if g == 0:
-            copy_down.wait()
-            copy_up.wait()
+            loads[4].wait()
+            loads[5].wait()
         work(g, gate_col)
     lax.fori_loop(1, GROUP, push_back, 0)
     await_rows(GROUPS - 1)
@@ -384,17 +394,20 @@
                 ring_copy(stream, steps)[2].wait_recv()
                 total = total + ring_recv[slot_of[stream, steps]].astype(F32)
         down_out[half * HALF:(half + 1) * HALF, :] = total.astype(BF16)
+    def landed(g, columns):
+        return jnp.dot(
+            landing[:, g * 128:g * 128 + ROWS],
+            rows2d[g * ROWS:(g + 1) * ROWS, columns],
+            preferred_element_type=F32,
+        )
+
+    for n in range(WIDTH // 256):
+        columns = slice(n * 256, (n + 1) * 256)
+        tok_sum[:, columns] = landed(0, columns) + landed(1, columns) + landed(2, columns)
     land(3)
     for n in range(WIDTH // 256):
         columns = slice(n * 256, (n + 1) * 256)
-        total = jnp.zeros((TOK, 256), F32)
-        for g in range(GROUPS):
-            total = total + jnp.dot(
-                landing[:, g * 128:g * 128 + ROWS],
-                rows2d[g * ROWS:(g + 1) * ROWS, columns],
-                preferred_element_type=F32,
-            )
-        tok_out[:, columns] = total.astype(BF16)
+        tok_out[:, columns] = (tok_sum[:, columns] + landed(3, columns)).astype(BF16)
     gates = 1.0 / (1.0 + jnp.exp(-logits_ref[...]))
     step_to_expert = jnp.where(
         step_between(me, iota((PEERS, PEERS), 1)) == iota((PEERS, PEERS), 0), 1.0, 0.0
@@ -412,17 +425,10 @@
         ring_copy(stream, s)[2].wait_send()
 
 
-def hand_over(tokens, logits, down, tok_out, logit_out, down_out, sems):
-    copies = [
-        pltpu.make_async_copy(source, target, sems.at[i])
-        for i, (source, target) in enumerate(
-            ((tokens, tok_out), (logits, logit_out), (down, down_out))
-        )
-    ]
-    for copy in copies:
-        copy.start()
-    for copy in copies:
-        copy.wait()
+def hand_over(tokens, logits, down, tok_out, logit_out, down_out):
+    tok_out[...] = tokens[...]
+    logit_out[...] = logits[...]
+    down_out[...] = down[...]
 
 
 def on_device(grad_out, router_logits, choices, pre_act, w_down, w_up):
@@ -436,11 +442,16 @@
             jax.ShapeDtypeStruct((PEERS, TOK), F32),
             jax.ShapeDtypeStruct((BLOCK, WIDTH), BF16),
         ),
-        in_specs=[vmem, vmem, vmem, vmem, anywhere, anywhere],
+        in_specs=[anywhere] * 6,
         out_specs=(vmem, vmem, vmem),
         scratch_shapes=[
+            pltpu.VMEM((PEERS, CAP), I32),
+            pltpu.VMEM((PEERS, TOK), F32),
+            pltpu.VMEM((TOK, WIDTH), BF16),
+            pltpu.VMEM((CAP, FF), BF16),
             pltpu.VMEM((FF, WIDTH), BF16),
             pltpu.VMEM((WIDTH, FF), BF16),
+            pltpu.VMEM((TOK, WIDTH), F32),
             pltpu.VMEM((FLAT * SUB, 128), F32),
             pltpu.VMEM((FLAT, SUB, 128), BF16),
             pltpu.VMEM((FLAT, SUB, 128), BF16),
@@ -463,13 +474,13 @@
             pltpu.VMEM((RING * BLOCK, WIDTH), BF16),
             pltpu.VMEM((14, HALF, WIDTH), BF16),
             pltpu.VMEM((14, HALF, WIDTH), BF16),
-            dma((2,)),
+            dma((6,)),
             dma, dma((GROUPS,)), dma, dma((GROUPS,)),
             dma, dma((GROUPS,)), dma, dma((GROUPS,)),
             dma, dma((RING,)), dma((14,)), dma((14,)),
         ],
         compiler_params=pltpu.CompilerParams(
-            collective_id=0, has_side_effects=True, vmem_limit_bytes=56 << 20
+            collective_id=0, has_side_effects=True, vmem_limit_bytes=60 << 20
         ),
         cost_estimate=pl.CostEstimate(
             flops=3 * 2 * CAP * FF * WIDTH, bytes_accessed=12 << 20, transcendentals=CAP * FF
@@ -479,10 +490,8 @@
     tokens, logits, down = pl.pallas_call(
         hand_over,
         out_shape=[jax.ShapeDtypeStruct(x.shape, x.dtype) for x in (tokens, logits, down)],
-        in_specs=[anywhere] * 3,
-        out_specs=[anywhere] * 3,
-        scratch_shapes=[dma((3,))],
-        compiler_params=pltpu.CompilerParams(vmem_limit_bytes=60 << 20),
+        in_specs=[vmem] * 3,
+        out_specs=[vmem] * 3,
         name="hand_over",
     )(tokens, logits, down)
     return tokens[None], logits.T[None], down[None]

time: 126 us -> 101 us (0.80)
  Pallas kernels: 125 us -> 99.5 us
    pallas_call x1, Pallas kernels: 25.9 us -> 2.04 us  [on_device(): pl.pallas_call(hand_over, out_shape=[jax.ShapeDtypeStruct(x.shape, x.dtyp...]
where the time goes in v2:
time: 101 us; the launch traced here: 100 us
  Pallas kernels  99.5 us (99%)
    pallas_call x1, Pallas kernels, on_device(): pl.pallas_call(kernel, out_shape=(jax.ShapeDtypeStruct((TOK, WIDTH), BF16...  97.5 us
    pallas_call x1, Pallas kernels, on_device(): pl.pallas_call(hand_over, out_shape=[jax.ShapeDtypeStruct(x.shape, x.dtyp...  2.04 us

profile of v2, /device:TPU:1, one launch (start us, length us, event | category | flops | bytes accessed | tf_op | source)
XLA Modules:
  0.0 100.2 jit_solution(11143429050970704364)
XLA Ops:
  0.6 97.5 %expert_backward.1 = (bf16[128,2048]{1,0:T(8,128)(2,1)}, f32[64,128]{1,0:T(8,128)}, bf16[64,2048]{1,0:T(8,128)(2,1)}) custom-call(s32[64,256]{1,0:T(8,128)} %bitcast.19, f32[64,128]{1,0:T(8,128)} %bitcast.20, bf16[128,2048]{1,0:T(8,128)(2,1)} %bitcast.15, bf16[256,1024]{1,0:T(8,128)(2,1)} %bitcast.16, bf16[1024,2048]{1,0:T(8,128)(2,1)} %bitcast.13, ...), custom_call_target="tpu_custom_call" | custom-call | flops 3221225472 | bytes 12582912 | tf_op jit(solution)/shard_map/expert_backward/pallas_call | solution.py:438
  98.1 2.0 %hand_over.1 = (bf16[128,2048]{1,0:T(8,128)(2,1)}, f32[64,128]{1,0:T(8,128)}, bf16[64,2048]{1,0:T(8,128)(2,1)}) custom-call(bf16[128,2048]{1,0:T(8,128)(2,1)} %get-tuple-element.9.tokens, f32[64,128]{1,0:T(8,128)} %get-tuple-element.10.logits, bf16[64,2048]{1,0:T(8,128)(2,1)} %get-tuple-element.11.down), custom_call_target="tpu_custom_call" | custom-call | tf_op jit(solution)/shard_map/hand_over/pallas_call | solution.py:490

commit v3 on v2

--- a/solution.py
+++ b/solution.py
@@ -295,7 +295,8 @@
             loads[4].wait()
             loads[5].wait()
         work(g, gate_col)
-    lax.fori_loop(1, GROUP, push_back, 0)
+        if g > 0:
+            lax.fori_loop(max(1, (g - 1) * GROUP), g * GROUP, push_back, 0)
     await_rows(GROUPS - 1)
     gate_col = arrive(GROUPS - 1)
 
@@ -329,8 +330,8 @@
     multiply(0)
     for j in range(RING):
         pair_copy(j).start()
+    lax.fori_loop((GROUPS - 2) * GROUP, (GROUPS - 1) * GROUP, push_back, 0)
     multiply(1)
-    lax.fori_loop(GROUP, (GROUPS - 1) * GROUP, push_back, 0)
 
     streams = ((0, 1, 4), (0, -1, 3), (1, 1, 3), (1, -1, 4))
     slot_of = {}

time: 101 us -> 101 us (level)
  no operation moved by 1% of the time
where the time goes in v3:
time: 101 us
  Pallas kernels  100 us (99%)
    pallas_call x1, Pallas kernels, on_device(): pl.pallas_call(kernel, out_shape=(jax.ShapeDtypeStruct((TOK, WIDTH), BF16...  98.2 us
    pallas_call x1, Pallas kernels, on_device(): pl.pallas_call(hand_over, out_shape=[jax.ShapeDtypeStruct(x.shape, x.dtyp...  2.04 us

profile of v3, /device:TPU:1, one launch (start us, length us, event | category | flops | bytes accessed | tf_op | source)
XLA Modules:
  0.0 100.9 jit_solution(12816992309289502018)
XLA Ops:
  0.6 98.2 %expert_backward.1 = (bf16[128,2048]{1,0:T(8,128)(2,1)}, f32[64,128]{1,0:T(8,128)}, bf16[64,2048]{1,0:T(8,128)(2,1)}) custom-call(s32[64,256]{1,0:T(8,128)} %bitcast.19, f32[64,128]{1,0:T(8,128)} %bitcast.20, bf16[128,2048]{1,0:T(8,128)(2,1)} %bitcast.15, bf16[256,1024]{1,0:T(8,128)(2,1)} %bitcast.16, bf16[1024,2048]{1,0:T(8,128)(2,1)} %bitcast.13, ...), custom_call_target="tpu_custom_call" | custom-call | flops 3221225472 | bytes 12582912 | tf_op jit(solution)/shard_map/expert_backward/pallas_call | solution.py:439
  98.8 2.0 %hand_over.1 = (bf16[128,2048]{1,0:T(8,128)(2,1)}, f32[64,128]{1,0:T(8,128)}, bf16[64,2048]{1,0:T(8,128)(2,1)}) custom-call(bf16[128,2048]{1,0:T(8,128)(2,1)} %get-tuple-element.9.tokens, f32[64,128]{1,0:T(8,128)} %get-tuple-element.10.logits, bf16[64,2048]{1,0:T(8,128)(2,1)} %get-tuple-element.11.down), custom_call_target="tpu_custom_call" | custom-call | tf_op jit(solution)/shard_map/hand_over/pallas_call | solution.py:491

commit v4 on v2

--- a/solution.py
+++ b/solution.py
@@ -93,7 +93,7 @@
         )
         return carry
 
-    lax.fori_loop(1, PEERS, greet, 0)
+    lax.fori_loop(1, PEERS, greet, 0, unroll=9)
     for other in (left, right, sibling):
         pl.semaphore_signal(barrier, inc=1, device_id={"dp": other}, device_id_type=MESH)
     loads = [
@@ -425,10 +425,17 @@
         ring_copy(stream, s)[2].wait_send()
 
 
-def hand_over(tokens, logits, down, tok_out, logit_out, down_out):
-    tok_out[...] = tokens[...]
-    logit_out[...] = logits[...]
-    down_out[...] = down[...]
+def hand_over(tokens, logits, down, tok_out, logit_out, down_out, sems):
+    copies = [
+        pltpu.make_async_copy(source, target, sems.at[i])
+        for i, (source, target) in enumerate(
+            ((tokens, tok_out), (logits, logit_out), (down, down_out))
+        )
+    ]
+    for copy in copies:
+        copy.start()
+    for copy in copies:
+        copy.wait()
 
 
 def on_device(grad_out, router_logits, choices, pre_act, w_down, w_up):
@@ -438,9 +445,9 @@
     tokens, logits, down = pl.pallas_call(
         kernel,
         out_shape=(
-            jax.ShapeDtypeStruct((TOK, WIDTH), BF16),
-            jax.ShapeDtypeStruct((PEERS, TOK), F32),
-            jax.ShapeDtypeStruct((BLOCK, WIDTH), BF16),
+            pltpu.VMEM((TOK, WIDTH), BF16),
+            pltpu.VMEM((PEERS, TOK), F32),
+            pltpu.VMEM((BLOCK, WIDTH), BF16),
         ),
         in_specs=[anywhere] * 6,
         out_specs=(vmem, vmem, vmem),
@@ -480,7 +487,7 @@
             dma, dma((RING,)), dma((14,)), dma((14,)),
         ],
         compiler_params=pltpu.CompilerParams(
-            collective_id=0, has_side_effects=True, vmem_limit_bytes=60 << 20
+            collective_id=0, has_side_effects=True, vmem_limit_bytes=54 << 20
         ),
         cost_estimate=pl.CostEstimate(
             flops=3 * 2 * CAP * FF * WIDTH, bytes_accessed=12 << 20, transcendentals=CAP * FF
@@ -491,7 +498,8 @@
         hand_over,
         out_shape=[jax.ShapeDtypeStruct(x.shape, x.dtype) for x in (tokens, logits, down)],
         in_specs=[vmem] * 3,
-        out_specs=[vmem] * 3,
+        out_specs=[anywhere] * 3,
+        scratch_shapes=[dma((3,))],
         name="hand_over",
     )(tokens, logits, down)
     return tokens[None], logits.T[None], down[None]

time: 101 us -> 104 us (1.030)
  local copies, waits for them, and re-layouts: 0 us -> 2.09 us
    unnamed x0 -> x6, local copies, waits for them, and re-layouts: none -> 2.09 us
where the time goes in v4:
time: 104 us; the launch traced here: 102 us
  Pallas kernels  99.4 us (96%)
  local copies, waits for them, and re-layouts  2.09 us (2%)
    pallas_call x1, Pallas kernels, on_device(): pl.pallas_call(kernel, out_shape=(pltpu.VMEM((TOK, WIDTH), BF16), pltpu.V...  97.3 us
    unnamed x6, local copies, waits for them, and re-layouts  2.09 us

profile of v4, /device:TPU:1, one launch (start us, length us, event | category | flops | bytes accessed | tf_op | source)
XLA Modules:
  0.0 102.3 jit_solution(15414822338068182005)
XLA Ops:
  0.6 97.3 %expert_backward.1 = (bf16[128,2048]{1,0:T(8,128)(2,1)S(1)}, f32[64,128]{1,0:T(8,128)S(1)}, bf16[64,2048]{1,0:T(8,128)(2,1)S(1)}) custom-call(s32[64,256]{1,0:T(8,128)} %bitcast.19, f32[64,128]{1,0:T(8,128)} %bitcast.20, bf16[128,2048]{1,0:T(8,128)(2,1)} %bitcast.15, bf16[256,1024]{1,0:T(8,128)(2,1)} %bitcast.16, bf16[1024,2048]{1,0:T(8,128)(2,1)} %bitcast.13, ...), custom_call_target="tpu_custom_call" | custom-call | flops 3221225472 | bytes 12582912 | tf_op jit(solution)/shard_map/expert_backward/pallas_call | solution.py:445
  98.0 0.0 copy-start
  98.0 0.8 copy-done
  98.8 0.0 copy-start.1
  98.8 0.7 copy-done.1
  99.5 0.0 copy-start.2
  99.5 0.6 copy-done.2
  100.1 2.0 %hand_over.1 = (bf16[128,2048]{1,0:T(8,128)(2,1)}, f32[64,128]{1,0:T(8,128)}, bf16[64,2048]{1,0:T(8,128)(2,1)}) custom-call(bf16[128,2048]{1,0:T(8,128)(2,1)} %copy-done, f32[64,128]{1,0:T(8,128)} %copy-done.2, bf16[64,2048]{1,0:T(8,128)(2,1)} %copy-done.1), custom_call_target="tpu_custom_call" | custom-call | tf_op jit(solution)/shard_map/hand_over/pallas_call | solution.py:497
Async XLA Ops:
  98.0 0.8 copy-start
  98.8 0.7 copy-start.1
  99.5 0.6 copy-start.2
